TPU v7x, 32 devices: a whole 2x2x4 slice. The times are simulated.
32 devices in a mesh: walk: 4 (over y, core), stretch: 8 (over z, x).
Axes of the slice: x: 2, y: 2, z: 4, core: 2. Of those that a mesh axis runs over, the one named last changes fastest.
Arguments:
- walkers: float32 [64, 48, 512], P(('walk', 'stretch')), may hold values from -6 to 6
- inverse_intersection: float32 [64, 48, 48], P(('walk', 'stretch')), may hold values from -0.875 to 0.875
- half_rotated: bfloat16 [1024, 48, 512], P('stretch'), may hold values from -0.076546554 to 0.076546554
- cholesky: bfloat16 [1024, 512, 512], P('stretch'), may hold values from -0.015625 to 0.015625
- field_noise: float32 [64, 1024], P('walk', 'stretch'), may hold values from -6 to 6
- branch_sources: int32 [64], P(('walk', 'stretch')), may hold values from 0 to 63, as said below
Outputs:
- force_bias: float32 [64, 1024], P('walk', 'stretch')
- exchange_energy: float32 [64], P(('walk', 'stretch'))
- new_walkers: float32 [64, 48, 512], P(('walk', 'stretch'))
Inputs may be any that keep to these rules, and one draw needn't show every extreme that they name: `branch_sources`: walker d lies in column (d // 2) % 8; every entry names a walker of the same column as its destination slot. A walker may be named by several slots or by none.
All inputs are finite; a program needn't handle non-finite values.
Results may differ from a plain program's by a relative error of at most 0.0029.
Values may be sent and summed in bfloat16 or wider, within the bound.
A program may use at most 320 MiB of HBM per device.

v0:
```python
import math

import jax
import jax.numpy as jnp
from jax import lax
from jax.sharding import PartitionSpec as P

ORDERS = 2


def apply_rows(psi_rows, field_rows, chol_flat, orbital_count):
    row_count = psi_rows.shape[0]
    occupied = psi_rows.shape[1]
    block_size = math.gcd(row_count, 16)
    blocks = row_count // block_size

    def one_block(operands):
        psi_block, field_block = operands
        matrix = jnp.dot(field_block, chol_flat, preferred_element_type=jnp.float32).reshape(
            block_size, orbital_count, orbital_count
        )
        return jnp.einsum(
            "bip,bpq->biq", psi_block.astype(jnp.float32), matrix, precision=lax.Precision.HIGHEST
        )

    result = lax.map(
        one_block,
        (
            psi_rows.reshape(blocks, block_size, occupied, orbital_count),
            field_rows.reshape(blocks, block_size, field_rows.shape[1]),
        ),
    )
    return result.reshape(row_count, occupied, orbital_count)


def shards(walkers, inverse_intersection, half_rotated, cholesky, field_noise, branch_sources):
    walker_count = walkers.shape[0]
    occupied = walkers.shape[1]
    orbital_count = walkers.shape[2]
    local_vectors = half_rotated.shape[0]
    group_size = walker_count * lax.axis_size("stretch")
    green_rows = jnp.einsum(
        "wij,wjp->wip", inverse_intersection, walkers, precision=lax.Precision.HIGHEST
    ).astype(jnp.bfloat16)
    hr_flat = half_rotated.reshape(local_vectors * occupied, orbital_count)
    initial = (
        jnp.zeros((group_size, local_vectors), jnp.float32),
        jnp.zeros((group_size,), jnp.float32),
    )
    visit_shard_rows = lax.all_gather(green_rows, "stretch", axis=0, tiled=True)
    row_count = visit_shard_rows.shape[0]
    intersections = lax.dot_general(
        hr_flat,
        visit_shard_rows.reshape(row_count * occupied, orbital_count),
        (((1,), (1,)), ((), ())),
        preferred_element_type=jnp.float32,
    )
    intersections = intersections.reshape(local_vectors, occupied, row_count, occupied)
    bias_block = 2.0 * jnp.trace(intersections, axis1=1, axis2=3).T
    energy_block = -0.5 * jnp.sum(
        intersections * jnp.transpose(intersections, (0, 3, 2, 1)), axis=(0, 1, 3)
    )
    force_bias = lax.dynamic_update_slice_in_dim(initial[0], bias_block, jnp.int32(0), 0)
    exchange_energy = lax.psum_scatter(energy_block, "stretch", scatter_dimension=0, tiled=True)
    fields = (0.05 * (field_noise - force_bias)).astype(jnp.bfloat16)
    chol_flat = cholesky.reshape(local_vectors, orbital_count * orbital_count)
    propagated = walkers
    psi_local = walkers.astype(jnp.bfloat16)
    for degree in range(1, ORDERS + 1):
        partial_terms = apply_rows(
            lax.all_gather(psi_local, "stretch", axis=0, tiled=True),
            fields,
            chol_flat,
            orbital_count,
        )
        summed = lax.psum_scatter(partial_terms, "stretch", scatter_dimension=0, tiled=True)
        term_local = summed / degree
        propagated = propagated + term_local
        psi_local = term_local.astype(jnp.bfloat16)
    column = lax.all_gather(propagated, "walk", axis=0, tiled=True)
    position = branch_sources // group_size * walker_count + branch_sources % walker_count
    picked = jnp.take(column, position, axis=0)
    return (force_bias, exchange_energy, picked)


def solution(mesh):
    placed = (
        P(("walk", "stretch"), None, None),
        P(("walk", "stretch"), None, None),
        P("stretch", None, None),
        P("stretch", None, None),
        P("walk", "stretch"),
        P(("walk", "stretch")),
    )
    return jax.shard_map(
        shards,
        mesh=mesh,
        in_specs=placed,
        out_specs=(
            P("walk", "stretch"),
            P(("walk", "stretch")),
            P(("walk", "stretch"), None, None),
        ),
        check_vma=False,
    )
```

profile of v0, /device:TPU:0, one launch (start us, length us, event | category | flops | bytes accessed | tf_op | source)
XLA Modules:
  0.0 633.0 jit_solution(13821597069704872714)
XLA Ops:
  7.2 0.0 copy-start
  7.2 0.0 reduce-scatter.3.cloned.1.call-start
  7.2 1.6 convert_element_type.18
  8.8 0.0 copy-done
  8.8 1.2 convolution_convert_fusion
  10.1 33.8 %all_gather.12 = bf16[16,48,512]{2,1,0:T(8,128)(2,1)S(1)} all-gather(bf16[2,48,512]{2,1,0:T(8,128)(2,1)S(1)} %convolution_convert_fusion), channel_id=1, replica_groups=mesh['walk'=4,'stretch'=8] {'stretch'}, dimensions={0}, use_global_device_ids=true | all-gather | bytes 884736 | tf_op jit(solution)/shard_map/all_gather | solution.py:50
  43.9 12.0 %convolution_bitcast_fusion = f32[6144,768]{0,1:T(8,128)} fusion(bf16[768,512]{1,0:T(8,128)(2,1)S(1)} %bitcast.28, bf16[6144,512]{1,0:T(8,128)(2,1)} %bitcast.29), kind=kOutput, calls=%fused_computation.8 | convolution fusion | flops 4831838208 | bytes 25952256 | tf_op jit(solution)/shard_map/dot_general | solution.py:52
  55.9 18.6 %copy.26 = f32[6144,768]{1,0:T(8,128)} copy(f32[6144,768]{0,1:T(8,128)} %convolution_bitcast_fusion) | data formatting | bytes 37748736 | tf_op jit(solution)/shard_map/dot_general | solution.py:52
  74.5 39.2 %reshape.44 = f32[128,48,16,48]{3,2,1,0:T(8,128)} reshape(f32[6144,768]{1,0:T(8,128)} %copy.26) | data formatting | bytes 37748736 | tf_op jit(solution)/shard_map/reshape | solution.py:58
  113.7 52.1 %copy.28 = f32[128,48,16,48]{1,2,3,0:T(8,128)} copy(f32[128,48,16,48]{3,2,1,0:T(8,128)} %reshape.44) | data formatting | bytes 37748736 | tf_op jit(solution)/shard_map/reshape | solution.py:58
  165.8 31.7 %fusion = (f32[16]{0:T(128)S(1)}, f32[128,16]{1,0:T(8,128)S(1)}) fusion(f32[128,48,16,48]{3,2,1,0:T(8,128)} %reshape.44, f32[128,48,16,48]{1,2,3,0:T(8,128)} %copy.28, pred[48,48]{1,0:T(8,128)(4,1)S(1)} %iota_compare_fusion), kind=kLoop, calls=%fused_computation.2 | loop fusion | flops 18872304 | bytes 37759296 | tf_op jit(solution)/shard_map/reduce_sum | solution.py:60
  197.5 0.1 copy.27
  197.5 0.0 copy-start.5
  197.6 59.6 %copy.32 = bf16[16,8,512,512]{3,1,2,0:T(8,128)(2,1)} copy(bf16[16,8,512,512]{3,2,1,0:T(8,128)(2,1)} %bitcast.10) | data formatting | bytes 134217728
  257.2 0.0 copy-start.4
  257.2 0.0 copy-start.6
  257.2 86.5 %copy.29 = bf16[262144,128]{1,0:T(8,128)(2,1)} copy(bf16[262144,128]{0,1:T(8,128)(2,1)} %bitcast.6) | data formatting | bytes 134217728 | tf_op jit(solution)/shard_map/while/body/eval_jaxpr/dot_general | solution.py:19
  343.7 0.0 copy-done.4
  343.7 32.3 %all_gather.13 = bf16[16,48,512]{2,1,0:T(8,128)(2,1)S(1)} all-gather(bf16[2,48,512]{2,1,0:T(8,128)(2,1)S(1)} %copy-done.4), channel_id=1, replica_groups=mesh['walk'=4,'stretch'=8] {'stretch'}, dimensions={0}, use_global_device_ids=true | all-gather | bytes 884736 | tf_op jit(solution)/shard_map/all_gather | solution.py:71
  376.0 0.0 copy-done.5
  376.0 0.0 copy-done.6
  376.0 32.0 %fusion.9 = f32[16,512,512]{2,0,1:T(8,128)} fusion(bf16[512,512,128]{2,1,0:T(8,128)(2,1)} %bitcast.7, f32[16,128]{1,0:T(8,128)S(1)} %copy-done.6, f32[16,128]{1,0:T(8,128)S(1)} %multiply_bitcast_fusion), kind=kOutput, calls=%fused_computation.17 | convolution fusion | flops 1073747968 | bytes 83902464 | tf_op jit(solution)/shard_map/while/body/eval_jaxpr/dot_general | solution.py:19
  408.0 0.0 copy-start.8
  408.0 0.0 copy-start.7
  408.0 0.0 copy-start.2
  408.0 0.0 copy-start.1
  408.0 22.0 %fusion.5 = f32[16,48,512]{2,1,0:T(8,128)} fusion(bf16[16,48,512]{2,1,0:T(8,128)(2,1)S(1)} %all_gather.13, f32[16,512,512]{2,0,1:T(8,128)} %fusion.9), kind=kOutput, calls=%fused_computation.9 | convolution fusion | flops 2415919104 | bytes 19136512 | tf_op jit(solution)/shard_map/while/body/eval_jaxpr/bip,bpq->biq/dot_general | solution.py:22
  430.0 0.0 reduce-scatter.3.cloned.1.call-update
  430.0 0.0 reduce-scatter.5.cloned.1.call-start
  430.0 65.9 %reduce-scatter.3.cloned.1.call-done = f32[2,48,512]{2,1,0:T(8,128)} async-done(((f32[16,48,512]{2,1,0:T(8,128)}), f32[2,48,512]{2,1,0:T(8,128)}) %reduce-scatter.3.cloned.1.call-update) | async-done | bytes 196624 | tf_op jit(solution)/shard_map/reduce_scatter | solution.py:76
  496.0 0.0 copy-start.3
  496.0 1.0 convert_element_type.19
  497.0 32.3 %all_gather.14 = bf16[16,48,512]{2,1,0:T(8,128)(2,1)S(1)} all-gather(bf16[2,48,512]{2,1,0:T(8,128)(2,1)S(1)} %convert_element_type.19), channel_id=1, replica_groups=mesh['walk'=4,'stretch'=8] {'stretch'}, dimensions={0}, use_global_device_ids=true | all-gather | bytes 884736 | tf_op jit(solution)/shard_map/all_gather | solution.py:71
  529.3 21.9 %fusion.1 = f32[16,48,512]{2,1,0:T(8,128)} fusion(bf16[16,48,512]{2,1,0:T(8,128)(2,1)S(1)} %all_gather.14, f32[16,512,512]{2,0,1:T(8,128)} %fusion.9), kind=kOutput, calls=%fused_computation.4 | convolution fusion | flops 2415919104 | bytes 19136512 | tf_op jit(solution)/shard_map/while/body/eval_jaxpr/bip,bpq->biq/dot_general | solution.py:22
  551.2 0.0 reduce-scatter.5.cloned.1.call-update
  551.2 19.4 %all-reduce = f32[16]{0:T(128)S(1)} all-reduce(f32[16]{0:T(128)S(1)} %broadcast_multiply_fusion), channel_id=2, replica_groups=mesh['walk'=4,'stretch'=8] {'stretch'}, use_global_device_ids=true, to_apply=%region_2.3.clone | all-reduce | flops 16 | bytes 128
  570.7 0.0 copy-done.8
  570.7 0.6 dynamic-slice.3
  571.9 0.6 dynamic-slice.4
  572.5 0.0 copy-done.7
  572.5 42.7 %reduce-scatter.5.cloned.1.call-done = f32[2,48,512]{2,1,0:T(8,128)} async-done(((f32[16,48,512]{2,1,0:T(8,128)}), f32[2,48,512]{2,1,0:T(8,128)}) %reduce-scatter.5.cloned.1.call-update) | async-done | bytes 196624 | tf_op jit(solution)/shard_map/reduce_scatter | solution.py:76
  615.3 0.0 copy-done.2
  615.3 0.0 copy-done.3
  615.3 1.0 multiply_add_fusion
  616.2 8.6 %all_gather.15 = f32[8,48,512]{2,1,0:T(8,128)S(1)} all-gather(f32[2,48,512]{2,1,0:T(8,128)S(1)} %multiply_add_fusion), channel_id=1, replica_groups=mesh['walk'=4,'stretch'=8] {'walk'}, dimensions={0}, use_global_device_ids=true | all-gather | bytes 983040 | tf_op jit(solution)/shard_map/all_gather | solution.py:80
  624.8 0.6 gather_fusion
  625.4 0.8 broadcast_select_fusion
  626.1 0.0 copy-done.1
  (5 shorter events, 0.0 us)
Async XLA Ops:
  7.2 1.7 copy-start
  7.2 488.8 %reduce-scatter.3.cloned.1.call-start = ((), (), s32[]{:S(2)}) async-start(), calls=%async_computation.2 | async-start | bytes 1769472 | tf_op jit(solution)/shard_map/reduce_scatter | solution.py:76
  197.5 178.4 %copy-start.5 = (f32[16,128]{1,0:T(8,128)}, f32[16,128]{1,0:T(8,128)S(1)}, u32[]{:S(2)}) copy-start(f32[16,128]{1,0:T(8,128)S(1)} %multiply_bitcast_fusion) | copy-start | bytes 24580
  257.2 86.5 %copy-start.4 = (bf16[2,48,512]{2,1,0:T(8,128)(2,1)S(1)}, bf16[2,48,512]{2,1,0:T(8,128)(2,1)}, u32[]{:S(2)}) copy-start(bf16[2,48,512]{2,1,0:T(8,128)(2,1)} %convert_element_type.18) | copy-start | bytes 294916
  257.2 118.8 %copy-start.6 = (f32[16,128]{1,0:T(8,128)S(1)}, f32[16,128]{1,0:T(8,128)}, u32[]{:S(2)}) copy-start(f32[16,128]{1,0:T(8,128)} %param.10) | copy-start | bytes 24580
  408.0 162.7 %copy-start.8 = (u32[32]{0:T(128)S(1)}, u32[32]{0:T(128)}, u32[]{:S(2)}) copy-start(u32[32]{0:T(128)} %constant.85) | copy-start | bytes 388
  408.0 164.5 %copy-start.7 = (s32[2]{0:T(128)S(1)}, s32[2]{0:T(128)}, u32[]{:S(2)}) copy-start(s32[2]{0:T(128)} %param.11) | copy-start | bytes 28
  408.0 207.3 %copy-start.2 = (f32[2,48,512]{2,1,0:T(8,128)S(1)}, f32[2,48,512]{2,1,0:T(8,128)}, u32[]{:S(2)}) copy-start(f32[2,48,512]{2,1,0:T(8,128)} %param.6) | copy-start | bytes 589828
  408.0 218.1 %copy-start.1 = (f32[2,48,48]{2,1,0:T(8,128)S(1)}, f32[2,48,48]{2,1,0:T(8,128)}, u32[]{:S(2)}) copy-start(f32[2,48,48]{2,1,0:T(8,128)} %param.7) | copy-start | bytes 55300
  430.0 185.3 %reduce-scatter.5.cloned.1.call-start = ((), (), s32[]{:S(2)}) async-start(), calls=%async_computation.3 | async-start | bytes 1769472 | tf_op jit(solution)/shard_map/reduce_scatter | solution.py:76
  496.0 119.3 %copy-start.3 = (f32[2,48,512]{2,1,0:T(8,128)S(1)}, f32[2,48,512]{2,1,0:T(8,128)}, u32[]{:S(2)}) copy-start(f32[2,48,512]{2,1,0:T(8,128)} %reduce-scatter.3.cloned.1.call-done) | copy-start | bytes 589828
Sparse Core Ops, SparseCore 0:
  430.1 65.7 reduce-scatter.2
  551.3 63.8 reduce-scatter.4
where the time goes:
time: 637 us; the launch traced here: 633 us
  local copies, waits for them, and re-layouts  258 us (41%)
  blocking collectives  126 us (20%)
  waiting for transfers between devices  109 us (17%)
  matrix products  89.1 us (14%)
  other arithmetic  36.1 us (6%)
  between operations  14.8 us (2%)
    reduce_scatter x2, waiting for transfers between devices, shards(): lax.psum_scatter(partial_terms, 'stretch', scatter_dimension=0, tiled=True)  109 us
    reshape x2, local copies, waits for them, and re-layouts, shards(): intersections.reshape(local_vectors, occupied, row_count, occupied)  91.3 us
    dot_general x1, local copies, waits for them, and re-layouts, one_block(): jnp.dot(field_block, chol_flat, preferred_element_type=jnp.float32)  86.5 us
    all_gather x2, blocking collectives, shards(): lax.all_gather(psi_local, 'stretch', axis=0, tiled=True)  64.6 us
    unnamed x21, local copies, waits for them, and re-layouts  60.8 us
    dot_general x2, matrix products, one_block(): jnp.einsum('bip,bpq->biq', psi_block.astype(jnp.float32), matrix, precisi...  43.9 us
    all_gather x1, blocking collectives, shards(): visit_shard_rows = lax.all_gather(green_rows, 'stretch', axis=0, tiled=True)  33.8 us
    dot_general x1, matrix products, one_block(): jnp.dot(field_block, chol_flat, preferred_element_type=jnp.float32)  32 us
  transfers between devices with their start and end apart: 2, of which 2 were waited for; matrix products, arithmetic and copies ran while one was open for 0% of the time, Pallas kernels for 0%

commit v1 on v0

v1 whole, which is shorter than its diff:
```python
import functools
import math

import jax
import jax.numpy as jnp
from jax import lax
from jax.experimental import pallas as pl
from jax.experimental.pallas import tpu as pltpu
from jax.sharding import PartitionSpec as P

ORDERS = 2
ROWS = 16
MESH = pl.DeviceIdType.MESH
VMEM = pltpu.VMEM
LIMIT = 60 * 2**20


def around(axis, n, me, d):
    return {axis: lax.rem(me + d, n)}


def send(src, dst, sems, stage, d, device):
    return pltpu.make_async_remote_copy(
        src_ref=src,
        dst_ref=dst,
        send_sem=sems[0].at[stage, d - 1],
        recv_sem=sems[1].at[stage, d - 1],
        device_id=device,
        device_id_type=MESH,
    )


def greet(axes):
    barrier = pltpu.get_barrier_semaphore()
    total = 0
    for axis, n, me in axes:
        for d in range(1, n):
            pl.semaphore_signal(barrier, inc=1, device_id=around(axis, n, me, d), device_id_type=MESH)
        total += n - 1
    pl.semaphore_wait(barrier, total)


def green_kernel(n, inverse_ref, walkers_ref, out_ref, mine, landed, send_sem, recv_sem):
    me = lax.axis_index("stretch")
    sems = (send_sem, recv_sem)
    for k in range(walkers_ref.shape[0]):
        mine[k] = jnp.dot(
            inverse_ref[k],
            walkers_ref[k],
            precision=lax.Precision.HIGHEST,
            preferred_element_type=jnp.float32,
        ).astype(jnp.bfloat16)
    greet([("stretch", n, me)])
    copies = []
    for d in range(1, n):
        copy = send(mine, landed.at[me], sems, 0, d, around("stretch", n, me, d))
        copy.start()
        copies.append(copy)
    out_ref[me] = mine[...]
    for d in range(1, n):
        copies[d - 1].wait()
        source = lax.rem(me - d + n, n)
        out_ref[source] = landed[source]


def gather_green(inverse, walkers, n):
    shape = walkers.shape
    return pl.pallas_call(
        functools.partial(green_kernel, n),
        out_shape=jax.ShapeDtypeStruct((n, *shape), jnp.bfloat16),
        in_specs=[pl.BlockSpec(memory_space=VMEM)] * 2,
        out_specs=pl.BlockSpec(memory_space=VMEM),
        scratch_shapes=[
            VMEM(shape, jnp.bfloat16),
            VMEM((n, *shape), jnp.bfloat16),
            pltpu.SemaphoreType.DMA((1, n - 1)),
            pltpu.SemaphoreType.DMA((1, n - 1)),
        ],
        compiler_params=pltpu.CompilerParams(
            collective_id=0, has_side_effects=True, vmem_limit_bytes=LIMIT
        ),
    )(inverse, walkers)


def bias_kernel(green_ref, rotated_ref, noise_ref, bias_ref, fields_ref, energy_ref, inter):
    step = pl.program_id(1)
    occupied, block, orbitals = green_ref.shape
    span, vectors, _ = rotated_ref.shape
    green = green_ref[...].reshape(occupied * block, orbitals)
    for i in range(0, span, 2):
        part = lax.dot_general(
            green,
            rotated_ref[i : i + 2].reshape(2 * vectors, orbitals),
            (((1,), (1,)), ((), ())),
            preferred_element_type=jnp.float32,
        )
        for k in range(2):
            inter[step * span + i + k] = part[:, k * vectors : (k + 1) * vectors].reshape(
                occupied, block, vectors
            )

    @pl.when(step == pl.num_programs(1) - 1)
    def _():
        def one(i, carry):
            energy, trace = carry
            energy = energy + jnp.sum(inter[i] * inter[:, i], axis=0)
            return energy, trace + inter[i, i]

        zero = jnp.zeros((block, vectors), jnp.float32)
        energy, trace = lax.fori_loop(0, occupied, one, (zero, zero))
        bias = 2.0 * trace
        bias_ref[...] = bias
        fields_ref[...] = (0.05 * (noise_ref[...] - bias)).astype(jnp.bfloat16).astype(jnp.float32)
        share = -0.5 * jnp.sum(energy, axis=1, keepdims=True)
        energy_ref[...] = jnp.broadcast_to(share[:, :, None], energy_ref.shape)


def bias_and_energy(green, rotated, noise):
    occupied, group, orbitals = green.shape
    vectors = rotated.shape[1]
    block = math.gcd(group, 16)
    span = 8
    grid = (group // block, occupied // span)
    return pl.pallas_call(
        bias_kernel,
        grid=grid,
        out_shape=(
            jax.ShapeDtypeStruct((group, vectors), jnp.float32),
            jax.ShapeDtypeStruct((group, vectors), jnp.float32),
            jax.ShapeDtypeStruct((group, 8, 128), jnp.float32),
        ),
        in_specs=[
            pl.BlockSpec((occupied, block, orbitals), lambda w, i: (0, w, 0)),
            pl.BlockSpec((span, vectors, orbitals), lambda w, i: (i, 0, 0)),
            pl.BlockSpec((block, vectors), lambda w, i: (w, 0)),
        ],
        out_specs=(
            pl.BlockSpec((block, vectors), lambda w, i: (w, 0)),
            pl.BlockSpec((block, vectors), lambda w, i: (w, 0)),
            pl.BlockSpec((block, 8, 128), lambda w, i: (w, 0, 0)),
        ),
        scratch_shapes=[VMEM((occupied, occupied, block, vectors), jnp.float32)],
        compiler_params=pltpu.CompilerParams(vmem_limit_bytes=LIMIT),
    )(green, rotated, noise)


def propagate_kernel(
    n,
    columns,
    fields_ref,
    energy_in,
    rows_ref,
    walkers_ref,
    chol_ref,
    out_ref,
    energy_ref,
    spread,
    matrix,
    rows_all,
    rows_next,
    outgoing,
    landed_one,
    landed_two,
    energy_landed,
    column_walkers,
    column_terms,
    terms,
    total,
    send_sem,
    recv_sem,
    column_send,
    column_recv,
):
    me = lax.axis_index("stretch")
    seat = lax.axis_index("walk")
    step = pl.program_id(0)
    last = pl.num_programs(0) - 1
    vectors, span, orbitals = chol_ref.shape
    group = fields_ref.shape[0]
    count = rows_ref.shape[0]
    sems = (send_sem, recv_sem)
    column_sems = (column_send, column_recv)

    def first_sends():
        copies = []
        for d in range(1, n):
            to = around("stretch", n, me, d)
            there = lax.rem(me + d, n)
            copies.append(send(rows_ref, rows_all.at[me], sems, 0, d, to))
            copies.append(send(energy_in.at[there], energy_landed.at[me], sems, 1, d, to))
        for d in range(1, columns):
            to = around("walk", columns, seat, d)
            copies.append(send(walkers_ref, column_walkers.at[seat], column_sems, 0, d, to))
        return copies

    @pl.when(step == 0)
    def _():
        greet([("stretch", n, me), ("walk", columns, seat)])
        for copy in first_sends():
            copy.start()
        wide = vectors * ROWS
        column = lax.broadcasted_iota(jnp.int32, (vectors, wide), 1)
        row = lax.broadcasted_iota(jnp.int32, (vectors, wide), 0)
        repeat = jnp.where(column // ROWS == row, 1.0, 0.0).astype(jnp.bfloat16)
        repeated = jnp.dot(
            fields_ref[...].astype(jnp.bfloat16), repeat, preferred_element_type=jnp.float32
        )
        place = lax.broadcasted_iota(jnp.int32, (ROWS, wide), 0)
        where = lax.broadcasted_iota(jnp.int32, (ROWS, wide), 1) % ROWS
        for w in range(group):
            line = jnp.broadcast_to(repeated[w : w + 1], (ROWS, wide))
            spread[w * ROWS : (w + 1) * ROWS] = jnp.where(place == where, line, 0.0).astype(
                jnp.bfloat16
            )

    for c in range(span // ROWS):
        product = jnp.dot(
            spread[...],
            chol_ref[:, c * ROWS : (c + 1) * ROWS, :].reshape(vectors * ROWS, orbitals),
            preferred_element_type=jnp.float32,
        )
        start = pl.multiple_of(step * span + c * ROWS, ROWS)
        matrix[:, pl.ds(start, ROWS), :] = product.astype(jnp.bfloat16).reshape(
            group, ROWS, orbitals
        )

    @pl.when(step == last)
    def _():
        def apply(rows, owner, k):
            return jnp.dot(
                rows[owner, k], matrix[owner * count + k], preferred_element_type=jnp.float32
            )

        for copy in first_sends():
            copy.wait()
        rows_all[me] = rows_ref[...]
        column_walkers[seat] = walkers_ref[...]
        energy = energy_in[me]
        for d in range(1, n):
            energy = energy + energy_landed[lax.rem(me - d + n, n)]
        energy_ref[...] = energy

        copies = []
        for d in range(1, n):
            owner = lax.rem(me + d, n)
            for k in range(count):
                outgoing[owner, k] = apply(rows_all, owner, k).astype(jnp.bfloat16)
            copy = send(
                outgoing.at[owner], landed_one.at[me], sems, 2, d, around("stretch", n, me, d)
            )
            copy.start()
            copies.append(copy)
        for k in range(count):
            total[k] = apply(rows_all, me, k)
        for d in range(1, n):
            copies[d - 1].wait()
            total[...] += landed_one[lax.rem(me - d + n, n)].astype(jnp.float32)
        rows_next[me] = total[...].astype(jnp.bfloat16)
        copies = []
        for d in range(1, n):
            copy = send(
                rows_next.at[me], rows_next.at[me], sems, 3, d, around("stretch", n, me, d)
            )
            copy.start()
            copies.append(copy)
        second = [0.5 * apply(rows_next, me, k) for k in range(count)]
        for k in range(count):
            total[k] += second[k]
        backs = []
        for d in range(1, n):
            copies[d - 1].wait()
            owner = lax.rem(me - d + n, n)
            for k in range(count):
                outgoing[owner, k] = (0.5 * apply(rows_next, owner, k)).astype(jnp.bfloat16)
            copy = send(
                outgoing.at[owner], landed_two.at[me], sems, 4, d, around("stretch", n, me, n - d)
            )
            copy.start()
            backs.append(copy)
        for d in range(1, n):
            backs[d - 1].wait()
            total[...] += landed_two[lax.rem(me + d, n)].astype(jnp.float32)
        terms[...] = total[...].astype(jnp.bfloat16)
        copies = []
        for d in range(1, columns):
            copy = send(
                terms,
                column_terms.at[seat],
                column_sems,
                1,
                d,
                around("walk", columns, seat, d),
            )
            copy.start()
            copies.append(copy)
        out_ref[seat] = walkers_ref[...] + total[...]
        for d in range(1, columns):
            copies[d - 1].wait()
            source = lax.rem(seat - d + columns, columns)
            out_ref[source] = column_walkers[source] + column_terms[source].astype(jnp.float32)


def propagate(fields, energy, walkers, cholesky, n, columns):
    count, occupied, orbitals = walkers.shape
    group, vectors = fields.shape
    span = 2 * ROWS
    shape = (count, occupied, orbitals)
    whole = pl.BlockSpec(memory_space=VMEM)
    half = jnp.bfloat16
    return pl.pallas_call(
        functools.partial(propagate_kernel, n, columns),
        grid=(orbitals // span,),
        out_shape=(
            jax.ShapeDtypeStruct((columns, *shape), jnp.float32),
            jax.ShapeDtypeStruct((count, 8, 128), jnp.float32),
        ),
        in_specs=[
            whole,
            whole,
            whole,
            whole,
            pl.BlockSpec((vectors, span, orbitals), lambda p: (0, p, 0)),
        ],
        out_specs=(whole, whole),
        scratch_shapes=[
            VMEM((group * ROWS, vectors * ROWS), half),
            VMEM((group, orbitals, orbitals), half),
            VMEM((n, *shape), half),
            VMEM((n, *shape), half),
            VMEM((n, *shape), half),
            VMEM((n, *shape), half),
            VMEM((n, *shape), half),
            VMEM((n, count, 8, 128), jnp.float32),
            VMEM((columns, *shape), jnp.float32),
            VMEM((columns, *shape), half),
            VMEM(shape, half),
            VMEM(shape, jnp.float32),
            pltpu.SemaphoreType.DMA((5, n - 1)),
            pltpu.SemaphoreType.DMA((5, n - 1)),
            pltpu.SemaphoreType.DMA((2, columns - 1)),
            pltpu.SemaphoreType.DMA((2, columns - 1)),
        ],
        compiler_params=pltpu.CompilerParams(
            collective_id=1, has_side_effects=True, vmem_limit_bytes=LIMIT
        ),
    )(
        fields,
        energy.reshape(n, count, 8, 128),
        walkers.astype(half),
        walkers,
        cholesky,
    )


def shards(walkers, inverse_intersection, half_rotated, cholesky, field_noise, branch_sources):
    count, occupied, orbitals = walkers.shape
    n = lax.axis_size("stretch")
    columns = lax.axis_size("walk")
    group = count * n
    green = gather_green(inverse_intersection, walkers, n)
    green = jnp.transpose(green.reshape(group, occupied, orbitals), (1, 0, 2))
    rotated = jnp.transpose(half_rotated, (1, 0, 2))
    force_bias, fields, energy = bias_and_energy(green, rotated, field_noise)
    column, energy = propagate(fields, energy, walkers, cholesky, n, columns)
    position = branch_sources // group * count + branch_sources % count
    picked = jnp.take(column.reshape(columns * count, occupied, orbitals), position, axis=0)
    return (force_bias, energy[:, 0, 0], picked)


def solution(mesh):
    placed = (
        P(("walk", "stretch"), None, None),
        P(("walk", "stretch"), None, None),
        P("stretch", None, None),
        P("stretch", None, None),
        P("walk", "stretch"),
        P(("walk", "stretch")),
    )
    return jax.shard_map(
        shards,
        mesh=mesh,
        in_specs=placed,
        out_specs=(
            P("walk", "stretch"),
            P(("walk", "stretch")),
            P(("walk", "stretch"), None, None),
        ),
        check_vma=False,
    )
```

time: 637 us -> 159 us (0.25)
  local copies, waits for them, and re-layouts: 258 us -> 14.4 us
  Pallas kernels: 0 us -> 142 us
  blocking collectives: 126 us -> 0 us
  waiting for transfers between devices: 109 us -> 0 us
  matrix products: 89.1 us -> 0 us
  other arithmetic: 36.1 us -> 1.44 us
  between operations: 14.8 us -> 0.67 us
    pallas_call x0 -> x3, Pallas kernels: none -> 142 us  [the longest x1 108 us: propagate(): pl.pallas_call(functools.partial(propagate_kernel, n, columns), grid=(orb...]
    reduce_scatter x2 -> x0, waiting for transfers between devices: 109 us -> none  [shards(): lax.psum_scatter(partial_terms, 'stretch', scatter_dimension=0, tiled=True)]
    all_gather x4 -> x0, blocking collectives: 107 us -> none  [the longest x2 64.6 us: shards(): lax.all_gather(psi_local, 'stretch', axis=0, tiled=True)]
    dot_general x2 -> x0, local copies, waits for them, and re-layouts: 105 us -> none  [the longest x1 86.5 us: one_block(): jnp.dot(field_block, chol_flat, preferred_element_type=jnp.float32)]
    dot_general x5 -> x0, matrix products: 89.1 us -> none  [the longest x2 43.9 us: one_block(): jnp.einsum('bip,bpq->biq', psi_block.astype(jnp.float32), matrix, precisi...]
    reshape x2 -> x1, local copies, waits for them, and re-layouts: 91.3 us -> 2.45 us  [shards(): green = jnp.transpose(green.reshape(group, occupied, orbitals), (1, 0, 2))]
    unnamed x21 -> x5, local copies, waits for them, and re-layouts: 60.8 us -> 8.97 us
    reduce_sum x1 -> x0, other arithmetic: 31.7 us -> none  [shards(): jnp.sum(intersections * jnp.transpose(intersections, (0, 3, 2, 1)), axis=...]
  transfers between devices with their start and end apart: 2 -> 0, of which waited for: 2 -> 0; matrix products, arithmetic and copies ran while one was open for 0% -> 0% of each run, Pallas kernels for 0% -> 0%
where the time goes in v1:
time: 159 us; the launch traced here: 158 us
  Pallas kernels  142 us (89%)
  local copies, waits for them, and re-layouts  14.4 us (9%)
    pallas_call x1, Pallas kernels, propagate(): pl.pallas_call(functools.partial(propagate_kernel, n, columns), grid=(orb...  108 us
    pallas_call x1, Pallas kernels, gather_green(): pl.pallas_call(functools.partial(green_kernel, n), out_shape=jax.ShapeDty...  20.9 us
    pallas_call x1, Pallas kernels, bias_and_energy(): pl.pallas_call(bias_kernel, grid=grid, out_shape=(jax.ShapeDtypeStruct((g...  12.2 us
    unnamed x5, local copies, waits for them, and re-layouts  8.97 us

profile of v1, /device:TPU:0, one launch (start us, length us, event | category | flops | bytes accessed | tf_op | source)
XLA Modules:
  0.0 158.0 jit_solution(10748675712823672635)
XLA Ops:
  0.6 20.9 %shard_map.85 = bf16[8,2,48,512]{3,2,1,0:T(8,128)(2,1)} custom-call(f32[2,48,48]{2,1,0:T(8,128)} %inverse_ref.1, f32[2,48,512]{2,1,0:T(8,128)} %walkers_ref.3), custom_call_target="tpu_custom_call" | custom-call | tf_op jit(solution)/shard_map/pallas_call | solution.py:68
  21.5 2.4 %copy.17 = bf16[16,48,512]{2,0,1:T(8,128)(2,1)} copy(bf16[16,48,512]{2,1,0:T(8,128)(2,1)} %bitcast.10) | data formatting | bytes 1572864 | tf_op jit(solution)/shard_map/reshape | solution.py:361
  24.0 9.0 %copy.16 = bf16[128,48,512]{2,0,1:T(8,128)(2,1)} copy(bf16[128,48,512]{2,1,0:T(8,128)(2,1)} %param.8) | data formatting | bytes 12582912 | tf_op args[2]
  33.0 0.0 copy-start
  33.0 12.2 %shard_map.86 = (f32[16,128]{1,0:T(8,128)}, f32[16,128]{1,0:T(8,128)}, f32[16,8,128]{2,1,0:T(8,128)}) custom-call(bf16[48,16,512]{2,1,0:T(8,128)(2,1)} %bitcast.11, bf16[48,128,512]{2,1,0:T(8,128)(2,1)} %bitcast.9, f32[16,128]{1,0:T(8,128)} %noise_ref.1), custom_call_target="tpu_custom_call" | custom-call | tf_op jit(solution)/shard_map/pallas_call | solution.py:124
  45.2 0.0 copy-done
  45.2 0.7 convert_element_type.3.rows_ref
  45.8 0.0 copy-start.1
  45.8 108.4 %shard_map.87 = (f32[4,2,48,512]{3,2,1,0:T(8,128)}, f32[2,8,128]{2,1,0:T(8,128)}) custom-call(f32[16,128]{1,0:T(8,128)} %get-tuple-element.9.fields_ref, f32[8,2,8,128]{3,2,1,0:T(8,128)} %bitcast.12, bf16[2,48,512]{2,1,0:T(8,128)(2,1)} %convert_element_type.3.rows_ref, f32[2,48,512]{2,1,0:T(8,128)} %walkers_ref.3, bf16[128,512,512]{2,1,0:T(8,128)(2,1)} %chol_ref.1), custom_call_target="tpu_custom_call" | custom-call | tf_op jit(solution)/shard_map/pallas_call | solution.py:310
  154.2 1.3 slice_reduce_fusion
  155.5 0.0 copy-done.1
  155.6 1.7 %gather_fusion = f32[2,48,512]{2,1,0:T(8,128)S(1)} fusion(f32[8,48,512]{2,1,0:T(8,128)} %bitcast.13, s32[1024]{0:T(1024)S(1)} %pad_clamp_fusion), kind=kCustom, calls=%fused_computation | custom fusion | bytes 393224 | tf_op jit(solution)/shard_map/jit(_take)/gather | solution.py:366
  157.3 0.8 broadcast_select_fusion
  (2 shorter events, 0.0 us)
Async XLA Ops:
  33.0 12.2 %copy-start = (f32[2,48,512]{2,1,0:T(8,128)S(1)}, f32[2,48,512]{2,1,0:T(8,128)}, u32[]{:S(2)}) copy-start(f32[2,48,512]{2,1,0:T(8,128)} %walkers_ref.3) | copy-start | bytes 589828
  45.8 109.7 %copy-start.1 = (s32[2]{0:T(128)S(1)}, s32[2]{0:T(128)}, u32[]{:S(2)}) copy-start(s32[2]{0:T(128)} %param.11) | copy-start | bytes 28

commit v2 on v1

v2 whole, which is shorter than its diff:
```python
import functools
import math

import jax
import jax.numpy as jnp
from jax import lax
from jax.experimental import pallas as pl
from jax.experimental.pallas import tpu as pltpu
from jax.sharding import PartitionSpec as P

ORDERS = 2
ROWS = 16
MESH = pl.DeviceIdType.MESH
VMEM = pltpu.VMEM
LIMIT = 60 * 2**20


def around(axis, n, me, d):
    return {axis: lax.rem(me + d, n)}


def send(src, dst, sems, stage, d, device):
    return pltpu.make_async_remote_copy(
        src_ref=src,
        dst_ref=dst,
        send_sem=sems[0].at[stage, d - 1],
        recv_sem=sems[1].at[stage, d - 1],
        device_id=device,
        device_id_type=MESH,
    )


def greet(axes):
    barrier = pltpu.get_barrier_semaphore()
    total = 0
    for axis, n, me in axes:
        for d in range(1, n):
            pl.semaphore_signal(barrier, inc=1, device_id=around(axis, n, me, d), device_id_type=MESH)
        total += n - 1
    pl.semaphore_wait(barrier, total)


class Ring:
    def __init__(self, n, send_sem, recv_sem):
        self.n, self.line = n, n // 2
        self.me = lax.axis_index("stretch")
        self.parity = lax.rem(self.me, 2)
        self.at = self.me // 2
        self.pair = self.me + 1 - 2 * self.parity
        self.sems = (send_sem, recv_sem)

    def ahead(self, d):
        return lax.rem(self.at + d, self.line)

    def back(self, d):
        return lax.rem(self.at - d + self.line, self.line)

    def own(self, j):
        return 2 * j + self.parity

    def other(self, j):
        return 2 * j + 1 - self.parity

    def copy(self, src, dst, stage, slot, to):
        return send(src, dst, self.sems, stage, slot + 1, {"stretch": to})

    def along(self, buf, stage, d):
        return self.copy(buf.at[self.me], buf.at[self.me], stage, d - 1, self.own(self.ahead(d)))

    def across(self, buf, stage):
        return self.copy(buf.at[self.me], buf.at[self.me], stage, self.line - 1, self.pair)

    def forward(self, buf, stage, d):
        source = self.own(self.back(d))
        return self.copy(buf.at[source], buf.at[source], stage, self.line - 1 + d, self.pair)

    def gather_start(self, buf, stage):
        for d in range(1, self.line):
            self.along(buf, stage, d).start()
        self.across(buf, stage).start()

    def gather_forward(self, buf, stage):
        for d in range(1, self.line):
            self.along(buf, stage, d).wait_recv()
            self.forward(buf, stage, d).start()

    def gather_finish(self, buf, stage):
        for d in range(1, self.line):
            self.along(buf, stage, d).wait_send()
        self.across(buf, stage).wait()
        for d in range(1, self.line):
            self.forward(buf, stage, d).wait()

    def first(self, bufs, stage, d):
        j = self.ahead(d)
        return self.copy(bufs[0].at[j], bufs[1].at[j], stage, d, self.pair)

    def second(self, bufs, stage, d):
        j = self.ahead(d)
        return self.copy(
            bufs[2].at[j], bufs[3].at[self.at], stage, self.line + d - 1, self.own(j)
        )

    def scatter_first(self, bufs, stage, partial):
        for d in [*range(1, self.line), 0]:
            j = self.ahead(d)
            for k, value in enumerate(partial(self.other(j))):
                bufs[0][j, k] = value.astype(bufs[0].dtype)
            self.first(bufs, stage, d).start()

    def scatter_second(self, bufs, stage, partial, total):
        for d in [*range(1, self.line), 0]:
            j = self.ahead(d)
            values = partial(self.own(j))
            self.first(bufs, stage, d).wait()
            for k, value in enumerate(values):
                value = value + bufs[1][j, k].astype(jnp.float32)
                if d:
                    bufs[2][j, k] = value.astype(bufs[2].dtype)
                else:
                    total[k] = value
            if d:
                self.second(bufs, stage, d).start()

    def scatter_last(self, bufs, stage, total):
        for d in range(1, self.line):
            self.second(bufs, stage, d).wait()
            total[...] += bufs[3][self.back(d)].astype(jnp.float32)


def green_kernel(
    n, inverse_ref, walkers_ref, rotated_ref, out_ref, turned_ref, landed, send_sem, recv_sem
):
    ring = Ring(n, send_sem, recv_sem)
    vectors, occupied, orbitals = rotated_ref.shape
    per_vector = math.gcd(vectors, ROWS)

    def turn(low, high):
        @pl.loop(low, high)
        def _(g):
            start = pl.multiple_of(g * per_vector, per_vector)
            for i in range(0, occupied, ROWS):
                block = rotated_ref[pl.ds(start, per_vector), i : i + ROWS, :]
                turned_ref[i : i + ROWS, pl.ds(start, per_vector), :] = jnp.swapaxes(block, 0, 1)

    for k in range(walkers_ref.shape[0]):
        landed[ring.me, k] = jnp.dot(
            inverse_ref[k],
            walkers_ref[k],
            precision=lax.Precision.HIGHEST,
            preferred_element_type=jnp.float32,
        ).astype(jnp.bfloat16)
    greet([("stretch", n, ring.me)])
    ring.gather_start(landed, 0)
    blocks = vectors // per_vector
    turn(0, blocks // 2)
    ring.gather_forward(landed, 0)
    turn(blocks // 2, blocks)
    ring.gather_finish(landed, 0)
    count = walkers_ref.shape[0]
    several = math.gcd(n, ROWS // math.gcd(count, ROWS))
    block = several * count
    for b in range(n // several):
        for i in range(0, occupied, ROWS):
            part = landed[b * several : (b + 1) * several, :, i : i + ROWS, :]
            out_ref[i : i + ROWS, b * block : (b + 1) * block, :] = jnp.swapaxes(
                part.reshape(block, ROWS, orbitals), 0, 1
            )


def gather_green(inverse, walkers, rotated, n):
    shape = walkers.shape
    vectors, occupied, orbitals = rotated.shape
    return pl.pallas_call(
        functools.partial(green_kernel, n),
        out_shape=(
            jax.ShapeDtypeStruct((occupied, n * shape[0], orbitals), jnp.bfloat16),
            jax.ShapeDtypeStruct((occupied, vectors, orbitals), jnp.bfloat16),
        ),
        in_specs=[pl.BlockSpec(memory_space=VMEM)] * 3,
        out_specs=(pl.BlockSpec(memory_space=VMEM), pl.BlockSpec(memory_space=VMEM)),
        scratch_shapes=[
            VMEM((n, *shape), jnp.bfloat16),
            pltpu.SemaphoreType.DMA((1, n - 1)),
            pltpu.SemaphoreType.DMA((1, n - 1)),
        ],
        compiler_params=pltpu.CompilerParams(
            collective_id=0, has_side_effects=True, vmem_limit_bytes=LIMIT
        ),
    )(inverse, walkers, rotated)


def bias_kernel(green_ref, rotated_ref, noise_ref, bias_ref, fields_ref, energy_ref, inter):
    step = pl.program_id(1)
    occupied, block, orbitals = green_ref.shape
    span, vectors, _ = rotated_ref.shape
    green = green_ref[...].reshape(occupied * block, orbitals)
    for i in range(0, span, 2):
        part = lax.dot_general(
            green,
            rotated_ref[i : i + 2].reshape(2 * vectors, orbitals),
            (((1,), (1,)), ((), ())),
            preferred_element_type=jnp.float32,
        )
        for k in range(2):
            inter[step * span + i + k] = part[:, k * vectors : (k + 1) * vectors].reshape(
                occupied, block, vectors
            )

    @pl.when(step == pl.num_programs(1) - 1)
    def _():
        def one(i, carry):
            energy, trace = carry
            energy = energy + jnp.sum(inter[i] * inter[:, i], axis=0)
            return energy, trace + inter[i, i]

        zero = jnp.zeros((block, vectors), jnp.float32)
        energy, trace = lax.fori_loop(0, occupied, one, (zero, zero))
        bias = 2.0 * trace
        bias_ref[...] = bias
        fields_ref[...] = (0.05 * (noise_ref[...] - bias)).astype(jnp.bfloat16).astype(jnp.float32)
        share = -0.5 * jnp.sum(energy, axis=1, keepdims=True)
        energy_ref[...] = jnp.broadcast_to(share[:, :, None], energy_ref.shape)


def bias_and_energy(green, rotated, noise):
    occupied, group, orbitals = green.shape
    vectors = rotated.shape[1]
    block = math.gcd(group, 16)
    span = 8
    grid = (group // block, occupied // span)
    return pl.pallas_call(
        bias_kernel,
        grid=grid,
        out_shape=(
            jax.ShapeDtypeStruct((group, vectors), jnp.float32),
            jax.ShapeDtypeStruct((group, vectors), jnp.float32),
            jax.ShapeDtypeStruct((group, 8, 128), jnp.float32),
        ),
        in_specs=[
            pl.BlockSpec((occupied, block, orbitals), lambda w, i: (0, w, 0)),
            pl.BlockSpec((span, vectors, orbitals), lambda w, i: (i, 0, 0)),
            pl.BlockSpec((block, vectors), lambda w, i: (w, 0)),
        ],
        out_specs=(
            pl.BlockSpec((block, vectors), lambda w, i: (w, 0)),
            pl.BlockSpec((block, vectors), lambda w, i: (w, 0)),
            pl.BlockSpec((block, 8, 128), lambda w, i: (w, 0, 0)),
        ),
        scratch_shapes=[VMEM((occupied, occupied, block, vectors), jnp.float32)],
        compiler_params=pltpu.CompilerParams(vmem_limit_bytes=LIMIT),
    )(green, rotated, noise)


def propagate_kernel(
    n,
    columns,
    fields_ref,
    energy_in,
    rows_ref,
    walkers_ref,
    chol_ref,
    out_ref,
    energy_ref,
    spread,
    matrix,
    rows_all,
    rows_next,
    out_first,
    landed_first,
    out_second,
    landed_second,
    total,
    energy_landed,
    column_walkers,
    column_terms,
    terms,
    send_sem,
    recv_sem,
    column_send,
    column_recv,
):
    ring = Ring(n, send_sem, recv_sem)
    me = ring.me
    seat = lax.axis_index("walk")
    half, step = pl.program_id(0), pl.program_id(1)
    last = pl.num_programs(1) - 1
    vectors, span, width = chol_ref.shape
    group = fields_ref.shape[0]
    count = rows_ref.shape[0]
    column_sems = (column_send, column_recv)

    def at(h, p):
        return pl.when((half == h) & (step == p))

    def energy_copy(d):
        there = lax.rem(me + d, n)
        return ring.copy(energy_in.at[there], energy_landed.at[me], 1, d - 1, there)

    def column_copy(src, dst, stage, d):
        return send(
            src, dst.at[seat], column_sems, stage, d, around("walk", columns, seat, d)
        )

    def bufs(q):
        return (out_first.at[q], landed_first.at[q], out_second.at[q], landed_second.at[q])

    def order_one(h):
        def partial(owner):
            return [
                jnp.dot(
                    rows_all[owner, k],
                    matrix[h, owner * count + k],
                    preferred_element_type=jnp.float32,
                )
                for k in range(count)
            ]

        return partial

    def order_two(h):
        def one(owner, k):
            return 0.5 * sum(
                jnp.dot(
                    rows_next[g, owner, k],
                    matrix[h, owner * count + k, g * width : (g + 1) * width, :],
                    preferred_element_type=jnp.float32,
                )
                for g in range(2)
            )

        return lambda owner: [one(owner, k) for k in range(count)]

    @at(0, 0)
    def _():
        greet([("stretch", n, me), ("walk", columns, seat)])
        rows_all[me] = rows_ref[...]
        ring.gather_start(rows_all, 0)
        for d in range(1, n):
            energy_copy(d).start()
        for d in range(1, columns):
            column_copy(walkers_ref, column_walkers, 0, d).start()
        wide = vectors * ROWS
        column = lax.broadcasted_iota(jnp.int32, (vectors, wide), 1)
        row = lax.broadcasted_iota(jnp.int32, (vectors, wide), 0)
        repeat = jnp.where(column // ROWS == row, 1.0, 0.0).astype(jnp.bfloat16)
        repeated = jnp.dot(
            fields_ref[...].astype(jnp.bfloat16), repeat, preferred_element_type=jnp.float32
        )
        place = lax.broadcasted_iota(jnp.int32, (ROWS, wide), 0)
        where = lax.broadcasted_iota(jnp.int32, (ROWS, wide), 1) % ROWS
        for w in range(group):
            line = jnp.broadcast_to(repeated[w : w + 1], (ROWS, wide))
            spread[w * ROWS : (w + 1) * ROWS] = jnp.where(place == where, line, 0.0).astype(
                jnp.bfloat16
            )

    for c in range(span // ROWS):
        product = jnp.dot(
            spread[...],
            chol_ref[:, c * ROWS : (c + 1) * ROWS, :].reshape(vectors * ROWS, width),
            preferred_element_type=jnp.float32,
        )
        start = pl.multiple_of(step * span + c * ROWS, ROWS)
        matrix[half, :, pl.ds(start, ROWS), :] = product.astype(jnp.bfloat16).reshape(
            group, ROWS, width
        )

    @at(0, last // 2)
    def _():
        ring.gather_forward(rows_all, 0)

    @at(0, last)
    def _():
        ring.gather_finish(rows_all, 0)
        ring.scatter_first(bufs(0), 2, order_one(0))

    @at(1, last // 3)
    def _():
        ring.scatter_second(bufs(0), 2, order_one(0), total.at[0])

    @at(1, last // 3 * 2)
    def _():
        ring.scatter_last(bufs(0), 2, total.at[0])
        rows_next[0, me] = total[0].astype(jnp.bfloat16)
        ring.gather_start(rows_next.at[0], 4)

    @at(1, last - 1)
    def _():
        ring.gather_forward(rows_next.at[0], 4)

    @at(1, last)
    def _():
        ring.scatter_first(bufs(1), 3, order_one(1))
        ring.gather_finish(rows_next.at[0], 4)
        ring.scatter_second(bufs(1), 3, order_one(1), total.at[1])
        ring.scatter_last(bufs(1), 3, total.at[1])
        rows_next[1, me] = total[1].astype(jnp.bfloat16)
        ring.gather_start(rows_next.at[1], 5)
        for d in range(1, n):
            energy_copy(d).wait()
        energy = energy_in[me]
        for d in range(1, n):
            energy = energy + energy_landed[lax.rem(me - d + n, n)]
        energy_ref[...] = energy
        for d in range(1, columns):
            column_copy(walkers_ref, column_walkers, 0, d).wait()
        column_walkers[seat] = walkers_ref[...]
        ring.gather_forward(rows_next.at[1], 5)
        ring.gather_finish(rows_next.at[1], 5)
        for h in range(2):
            ring.scatter_first(bufs(2 + h), 6 + h, order_two(h))
        for h in range(2):
            ring.scatter_second(bufs(2 + h), 6 + h, order_two(h), total.at[2 + h])
        for h in range(2):
            ring.scatter_last(bufs(2 + h), 6 + h, total.at[2 + h])
            total[2 + h] += total[h]
            terms[h] = total[2 + h].astype(jnp.bfloat16)
            for d in range(1, columns):
                column_copy(terms.at[h], column_terms.at[h], 1 + h, d).start()
        for h in range(2):
            part = slice(h * width, (h + 1) * width)
            out_ref[seat, :, :, part] = walkers_ref[:, :, part] + total[2 + h]
            for d in range(1, columns):
                column_copy(terms.at[h], column_terms.at[h], 1 + h, d).wait()
                source = lax.rem(seat - d + columns, columns)
                out_ref[source, :, :, part] = column_walkers[source, :, :, part] + column_terms[
                    h, source
                ].astype(jnp.float32)


def propagate(fields, energy, walkers, cholesky, n, columns):
    count, occupied, orbitals = walkers.shape
    group, vectors = fields.shape
    span = 4 * ROWS
    width = orbitals // 2
    shape = (count, occupied, orbitals)
    part = (count, occupied, width)
    whole = pl.BlockSpec(memory_space=VMEM)
    half = jnp.bfloat16
    return pl.pallas_call(
        functools.partial(propagate_kernel, n, columns),
        grid=(2, orbitals // span),
        out_shape=(
            jax.ShapeDtypeStruct((columns, *shape), jnp.float32),
            jax.ShapeDtypeStruct((count, 8, 128), jnp.float32),
        ),
        in_specs=[
            whole,
            whole,
            whole,
            whole,
            pl.BlockSpec((vectors, span, width), lambda h, p: (0, p, h)),
        ],
        out_specs=(whole, whole),
        scratch_shapes=[
            VMEM((group * ROWS, vectors * ROWS), half),
            VMEM((2, group, orbitals, width), half),
            VMEM((n, *shape), half),
            VMEM((2, n, *part), half),
            VMEM((4, n // 2, *part), half),
            VMEM((4, n // 2, *part), half),
            VMEM((4, n // 2, *part), half),
            VMEM((4, n // 2, *part), half),
            VMEM((4, *part), jnp.float32),
            VMEM((n, count, 8, 128), jnp.float32),
            VMEM((columns, *shape), jnp.float32),
            VMEM((2, columns, *part), half),
            VMEM((2, *part), half),
            pltpu.SemaphoreType.DMA((8, n - 1)),
            pltpu.SemaphoreType.DMA((8, n - 1)),
            pltpu.SemaphoreType.DMA((3, columns - 1)),
            pltpu.SemaphoreType.DMA((3, columns - 1)),
        ],
        compiler_params=pltpu.CompilerParams(
            collective_id=1, has_side_effects=True, vmem_limit_bytes=LIMIT
        ),
    )(
        fields,
        energy.reshape(n, count, 8, 128),
        walkers.astype(half),
        walkers,
        cholesky,
    )


def shards(walkers, inverse_intersection, half_rotated, cholesky, field_noise, branch_sources):
    count, occupied, orbitals = walkers.shape
    n = lax.axis_size("stretch")
    columns = lax.axis_size("walk")
    group = count * n
    green, rotated = gather_green(inverse_intersection, walkers, half_rotated, n)
    force_bias, fields, energy = bias_and_energy(green, rotated, field_noise)
    column, energy = propagate(fields, energy, walkers, cholesky, n, columns)
    position = branch_sources // group * count + branch_sources % count
    column = column.reshape(columns * count, occupied, orbitals)
    picked = column.at[position].get(mode="promise_in_bounds")
    return (force_bias, energy[:, 0, 0], picked)


def solution(mesh):
    placed = (
        P(("walk", "stretch"), None, None),
        P(("walk", "stretch"), None, None),
        P("stretch", None, None),
        P("stretch", None, None),
        P("walk", "stretch"),
        P(("walk", "stretch")),
    )
    return jax.shard_map(
        shards,
        mesh=mesh,
        in_specs=placed,
        out_specs=(
            P("walk", "stretch"),
            P(("walk", "stretch")),
            P(("walk", "stretch"), None, None),
        ),
        check_vma=False,
    )
```

time: 159 us -> 118 us (0.74)
  Pallas kernels: 142 us -> 112 us
  local copies, waits for them, and re-layouts: 14.4 us -> 3.68 us
    pallas_call x2, Pallas kernels: 129 us -> 100 us  [the longest x1 74.8 us: propagate(): pl.pallas_call(functools.partial(propagate_kernel, n, columns), grid=(2,...]
    unnamed x5 -> x4, local copies, waits for them, and re-layouts: 8.97 us -> 0.01 us
    reshape x1 -> x0, local copies, waits for them, and re-layouts: 2.45 us -> none  [shards(): green = jnp.transpose(green.reshape(group, occupied, orbitals), (1, 0, 2))]
where the time goes in v2:
time: 118 us; the launch traced here: 117 us
  Pallas kernels  112 us (95%)
  local copies, waits for them, and re-layouts  3.68 us (3%)
    pallas_call x1, Pallas kernels, propagate(): pl.pallas_call(functools.partial(propagate_kernel, n, columns), grid=(2,...  74.8 us
    pallas_call x1, Pallas kernels, gather_green(): pl.pallas_call(functools.partial(green_kernel, n), out_shape=(jax.ShapeDt...  25.2 us
    pallas_call x1, Pallas kernels, bias_and_energy(): pl.pallas_call(bias_kernel, grid=grid, out_shape=(jax.ShapeDtypeStruct((g...  12.2 us
    gather x1, local copies, waits for them, and re-layouts, shards(): picked = column.at[position].get(mode='promise_in_bounds')  2.37 us

profile of v2, /device:TPU:0, one launch (start us, length us, event | category | flops | bytes accessed | tf_op | source)
XLA Modules:
  0.0 117.2 jit_solution(4623827463142534238)
XLA Ops:
  0.6 0.0 copy-start
  0.6 25.2 %shard_map.85 = (bf16[48,16,512]{2,1,0:T(8,128)(2,1)}, bf16[48,128,512]{2,1,0:T(8,128)(2,1)}) custom-call(f32[2,48,48]{2,1,0:T(8,128)} %inverse_ref.1, f32[2,48,512]{2,1,0:T(8,128)} %walkers_ref.3, bf16[128,48,512]{2,1,0:T(8,128)(2,1)} %rotated_ref.1), custom_call_target="tpu_custom_call" | custom-call | tf_op jit(solution)/shard_map/pallas_call | solution.py:174
  25.9 12.2 %shard_map.86 = (f32[16,128]{1,0:T(8,128)}, f32[16,128]{1,0:T(8,128)}, f32[16,8,128]{2,1,0:T(8,128)}) custom-call(bf16[48,16,512]{2,1,0:T(8,128)(2,1)} %get-tuple-element.10.green_ref, bf16[48,128,512]{2,1,0:T(8,128)(2,1)} %get-tuple-element.11.rotated_ref, f32[16,128]{1,0:T(8,128)} %noise_ref.1), custom_call_target="tpu_custom_call" | custom-call | tf_op jit(solution)/shard_map/pallas_call | solution.py:232
  38.1 0.0 copy-done
  38.1 0.7 convert_element_type.3.rows_ref
  38.7 0.0 copy-start.1
  38.7 74.8 %shard_map.87 = (f32[4,2,48,512]{3,2,1,0:T(8,128)}, f32[2,8,128]{2,1,0:T(8,128)}) custom-call(f32[16,128]{1,0:T(8,128)} %get-tuple-element.13.fields_ref, f32[8,2,8,128]{3,2,1,0:T(8,128)} %bitcast.2, bf16[2,48,512]{2,1,0:T(8,128)(2,1)} %convert_element_type.3.rows_ref, f32[2,48,512]{2,1,0:T(8,128)} %walkers_ref.3, bf16[128,512,512]{2,1,0:T(8,128)(2,1)} %chol_ref.1), custom_call_target="tpu_custom_call" | custom-call | tf_op jit(solution)/shard_map/pallas_call | solution.py:441
  113.5 0.0 copy-done.1
  113.5 2.4 %gather_fusion = f32[2,48,512]{2,1,0:T(8,128)} fusion(f32[8,48,512]{2,1,0:T(8,128)} %bitcast.3, s32[1024]{0:T(1024)S(1)} %pad_clamp_fusion), kind=kCustom, calls=%fused_computation | custom fusion | bytes 393224 | tf_op jit(solution)/shard_map/gather | solution.py:497
  115.9 1.3 %slice_reduce_fusion = f32[2]{0:T(128)} fusion(f32[2,8,128]{2,1,0:T(8,128)} %get-tuple-element.15), kind=kLoop, calls=%fused_computation.5 | loop fusion | bytes 16 | tf_op jit(solution)/shard_map/slice | solution.py:498
  (2 shorter events, 0.0 us)
Async XLA Ops:
  0.6 37.4 %copy-start = (f32[2,48,512]{2,1,0:T(8,128)S(1)}, f32[2,48,512]{2,1,0:T(8,128)}, u32[]{:S(2)}) copy-start(f32[2,48,512]{2,1,0:T(8,128)} %walkers_ref.3) | copy-start | bytes 589828
  38.7 74.8 %copy-start.1 = (s32[2]{0:T(128)S(1)}, s32[2]{0:T(128)}, u32[]{:S(2)}) copy-start(s32[2]{0:T(128)} %param.11) | copy-start | bytes 28
